TPU v7x, 32 devices: a whole 2x2x4 slice. The times are simulated.
32 devices in a mesh: dp: 8 (over z, y), mp: 4 (over x, core).
Axes of the slice: x: 2, y: 2, z: 4, core: 2. Of those that a mesh axis runs over, the one named last changes fastest.
Arguments:
- tokens: bfloat16 [128, 8192], P('dp', 'mp'), may hold values from -6 to 6
- gate_weight: bfloat16 [8192, 21504], P('mp', 'dp'), may hold values from -0.0625 to 0.0625
- up_weight: bfloat16 [8192, 21504], P('mp', 'dp'), may hold values from -0.0625 to 0.0625
- down_weight: bfloat16 [21504, 8192], P('dp', 'mp'), may hold values from -0.0390625 to 0.0390625
Outputs:
- mixed_out: bfloat16 [128, 8192], P('dp', 'mp')
All inputs are finite; a program needn't handle non-finite values.
Results may differ from a plain program's by a relative error of at most 0.005.
Values may be sent and summed in bfloat16 or wider, within the bound.
A program may use at most 128 MiB of HBM per device.

v0:
```python
import jax
import jax.numpy as jnp
from jax import lax
from jax.sharding import PartitionSpec as P


def swiglu(sums):
    return (jax.nn.silu(sums[:, 0, :]) * sums[:, 1, :]).astype(jnp.bfloat16)


def shards(tokens, gate_weight, up_weight, down_weight):
    paired = jnp.stack((gate_weight, up_weight), axis=1)
    partial_sums = jnp.einsum(
        "td,dkf->tkf",
        lax.all_gather(tokens, "dp", axis=0, tiled=True),
        paired,
        preferred_element_type=jnp.float32,
    )
    totals = lax.psum(partial_sums, "mp")
    hidden = swiglu(totals)
    mixed_out = lax.psum_scatter(
        jnp.dot(hidden, down_weight, preferred_element_type=jnp.float32),
        "dp",
        scatter_dimension=0,
        tiled=True,
    )
    return mixed_out.astype(jnp.bfloat16)


def solution(mesh):
    return jax.shard_map(
        shards,
        mesh=mesh,
        in_specs=(P("dp", "mp"), P("mp", "dp"), P("mp", "dp"), P("dp", "mp")),
        out_specs=P("dp", "mp"),
        check_vma=False,
    )
```

profile of v0, /device:TPU:0, one launch (start us, length us, event | category | flops | bytes accessed | tf_op | source)
XLA Modules:
  0.0 223.8 jit_solution(7592698520532821649)
XLA Ops:
  6.5 0.0 all-reduce.2.cloned.1.call-start
  6.5 33.2 %all_gather.3 = bf16[128,2048]{1,0:T(8,128)(2,1)S(1)} all-gather(bf16[16,2048]{1,0:T(8,128)(2,1)} %param.4), channel_id=1, replica_groups=mesh['dp'=8,'mp'=4] {'dp'}, dimensions={0}, use_global_device_ids=true | all-gather | bytes 589824 | tf_op jit(solution)/shard_map/all_gather | solution.py:15
  39.7 14.7 %copy.5 = bf16[2048,2688]{0,1:T(8,128)(2,1)} copy(bf16[2048,2688]{1,0:T(8,128)(2,1)} %param.5) | data formatting | bytes 22020096 | tf_op args[1]
  54.5 14.7 %copy.6 = bf16[2048,2688]{0,1:T(8,128)(2,1)} copy(bf16[2048,2688]{1,0:T(8,128)(2,1)} %param.6) | data formatting | bytes 22020096 | tf_op args[2]
  69.2 11.4 %fusion.4 = f32[128,2,2688]{0,2,1:T(8,128)} fusion(bf16[2048,1,2688]{0,2,1:T(8,128)(2,1)} %bitcast.21, bf16[2048,1,2688]{0,2,1:T(8,128)(2,1)} %bitcast.20, bf16[128,2048]{1,0:T(8,128)(2,1)S(1)} %all_gather.3), kind=kOutput, calls=%fused_computation.4 | convolution fusion | flops 2829582336 | bytes 25296896 | tf_op jit(solution)/shard_map/td,dkf->tkf/dot_general | solution.py:13
  80.7 0.0 all-reduce.2.cloned.1.call-update
  80.7 0.0 reduce-scatter.2.cloned.1.call-start
  80.7 63.3 %all-reduce.2.cloned.1.call-done = f32[128,2,2688]{0,2,1:T(8,128)} async-done(((f32[128,2,2688]{0,2,1:T(8,128)}), f32[128,2,2688]{0,2,1:T(8,128)}) %all-reduce.2.cloned.1.call-update) | async-done | bytes 2752528 | tf_op jit(solution)/shard_map/psum | solution.py:19
  144.0 7.7 %fusion.9 = f32[128,2048]{1,0:T(8,128)} fusion(bf16[2688,2048]{1,0:T(8,128)(2,1)} %param.7, f32[128,2,2688]{0,2,1:T(8,128)} %all-reduce.2.cloned.1.call-done), kind=kOutput, calls=%fused_computation.9 | convolution fusion | flops 1411350528 | bytes 14811136 | tf_op jit(solution)/shard_map/dot_general | solution.py:22
  151.7 0.0 reduce-scatter.2.cloned.1.call-update
  151.7 63.8 %reduce-scatter.2.cloned.1.call-done = f32[16,2048]{1,0:T(8,128)} async-done(((f32[128,2048]{1,0:T(8,128)}), f32[16,2048]{1,0:T(8,128)}) %reduce-scatter.2.cloned.1.call-update) | async-done | bytes 131088 | tf_op jit(solution)/shard_map/reduce_scatter | solution.py:21
  215.4 1.5 convert_element_type.7
Async XLA Ops:
  6.5 137.5 %all-reduce.2.cloned.1.call-start = ((), (), s32[]{:S(2)}) async-start(), calls=%async_computation.1 | async-start | bytes 5505024 | tf_op jit(solution)/shard_map/psum | solution.py:19
  80.7 134.8 %reduce-scatter.2.cloned.1.call-start = ((), (), s32[]{:S(2)}) async-start(), calls=%async_computation.2 | async-start | bytes 1179648 | tf_op jit(solution)/shard_map/reduce_scatter | solution.py:21
Sparse Core Ops, SparseCore 0:
  80.8 63.1 all-reduce.1
  151.8 63.5 reduce-scatter.1
where the time goes:
time: 225 us; the launch traced here: 224 us
  waiting for transfers between devices  127 us (56%)
  blocking collectives  33.2 us (15%)
  local copies, waits for them, and re-layouts  29.5 us (13%)
  matrix products  19.1 us (8%)
  between operations  13.4 us (6%)
    reduce_scatter x1, waiting for transfers between devices, shards(): lax.psum_scatter(jnp.dot(hidden, down_weight, preferred_element_type=jnp....  63.8 us
    psum x1, waiting for transfers between devices, shards(): totals = lax.psum(partial_sums, 'mp')  63.3 us
    all_gather x1, blocking collectives, shards(): lax.all_gather(tokens, 'dp', axis=0, tiled=True)  33.2 us
    unnamed x2, local copies, waits for them, and re-layouts  29.5 us
    dot_general x1, matrix products, shards(): jnp.einsum('td,dkf->tkf', lax.all_gather(tokens, 'dp', axis=0, tiled=True...  11.4 us
    dot_general x1, matrix products, shards(): jnp.dot(hidden, down_weight, preferred_element_type=jnp.float32)  7.67 us
  transfers between devices with their start and end apart: 2, of which 2 were waited for; matrix products, arithmetic and copies ran while one was open for 0% of the time, Pallas kernels for 0%

commit v1 on v0

--- a/solution.py
+++ b/solution.py
@@ -16,7 +16,7 @@
         paired,
         preferred_element_type=jnp.float32,
     )
-    totals = lax.psum(partial_sums, "mp")
+    totals = jnp.sum(lax.all_gather(partial_sums, "mp"), axis=0)
     hidden = swiglu(totals)
     mixed_out = lax.psum_scatter(
         jnp.dot(hidden, down_weight, preferred_element_type=jnp.float32),

time: 225 us -> 278 us (1.24)
  other arithmetic: 1.54 us -> 29.2 us
  local copies, waits for them, and re-layouts: 29.5 us -> 42.8 us
  waiting for transfers between devices: 127 us -> 139 us
    all_gather x0 -> x1, waiting for transfers between devices: none -> 75.9 us  [shards(): totals = jnp.sum(lax.all_gather(partial_sums, 'mp'), axis=0)]
    psum x1 -> x0, waiting for transfers between devices: 63.3 us -> none  [shards(): totals = lax.psum(partial_sums, 'mp')]
    reduce_sum x0 -> x1, other arithmetic: none -> 27.6 us  [shards(): totals = jnp.sum(lax.all_gather(partial_sums, 'mp'), axis=0)]
    all_gather x0 -> x1, local copies, waits for them, and re-layouts: none -> 13.4 us  [shards(): totals = jnp.sum(lax.all_gather(partial_sums, 'mp'), axis=0)]
where the time goes in v1:
time: 278 us; the launch traced here: 276 us
  waiting for transfers between devices  139 us (50%)
  local copies, waits for them, and re-layouts  42.8 us (15%)
  blocking collectives  33.2 us (12%)
  other arithmetic  29.2 us (11%)
  matrix products  18.3 us (7%)
  between operations  13.4 us (5%)
    all_gather x1, waiting for transfers between devices, shards(): totals = jnp.sum(lax.all_gather(partial_sums, 'mp'), axis=0)  75.9 us
    reduce_scatter x1, waiting for transfers between devices, shards(): lax.psum_scatter(jnp.dot(hidden, down_weight, preferred_element_type=jnp....  63.6 us
    all_gather x1, blocking collectives, shards(): lax.all_gather(tokens, 'dp', axis=0, tiled=True)  33.2 us
    unnamed x2, local copies, waits for them, and re-layouts  29.5 us
    reduce_sum x1, other arithmetic, shards(): totals = jnp.sum(lax.all_gather(partial_sums, 'mp'), axis=0)  27.6 us
    all_gather x1, local copies, waits for them, and re-layouts, shards(): totals = jnp.sum(lax.all_gather(partial_sums, 'mp'), axis=0)  13.4 us
    dot_general x1, matrix products, shards(): jnp.einsum('td,dkf->tkf', lax.all_gather(tokens, 'dp', axis=0, tiled=True...  11.4 us
    dot_general x1, matrix products, shards(): jnp.dot(hidden, down_weight, preferred_element_type=jnp.float32)  6.84 us
  transfers between devices with their start and end apart: 2, of which 2 were waited for; matrix products, arithmetic and copies ran while one was open for 0% of the time, Pallas kernels for 0%

profile of v1, /device:TPU:0, one launch (start us, length us, event | category | flops | bytes accessed | tf_op | source)
XLA Modules:
  0.0 276.4 jit_solution(16996834181343395410)
XLA Ops:
  6.5 0.0 all-gather.3.cloned.1.call-start
  6.5 33.2 %all_gather.9 = bf16[128,2048]{1,0:T(8,128)(2,1)S(1)} all-gather(bf16[16,2048]{1,0:T(8,128)(2,1)} %param.4), channel_id=1, replica_groups=mesh['dp'=8,'mp'=4] {'dp'}, dimensions={0}, use_global_device_ids=true | all-gather | bytes 589824 | tf_op jit(solution)/shard_map/all_gather | solution.py:15
  39.7 14.7 %copy.8 = bf16[2048,2688]{0,1:T(8,128)(2,1)} copy(bf16[2048,2688]{1,0:T(8,128)(2,1)} %param.5) | data formatting | bytes 22020096 | tf_op args[1]
  54.5 14.7 %copy.9 = bf16[2048,2688]{0,1:T(8,128)(2,1)} copy(bf16[2048,2688]{1,0:T(8,128)(2,1)} %param.6) | data formatting | bytes 22020096 | tf_op args[2]
  69.2 11.4 %fusion.4 = f32[128,2,2688]{0,2,1:T(8,128)} fusion(bf16[2048,1,2688]{0,2,1:T(8,128)(2,1)} %bitcast.23, bf16[2048,1,2688]{0,2,1:T(8,128)(2,1)} %bitcast.22, bf16[128,2048]{1,0:T(8,128)(2,1)S(1)} %all_gather.9), kind=kOutput, calls=%fused_computation.4 | convolution fusion | flops 2829582336 | bytes 25296896 | tf_op jit(solution)/shard_map/td,dkf->tkf/dot_general | solution.py:13
  80.7 0.0 all-gather.3.cloned.1.call-update
  80.7 0.0 reduce-scatter.2.cloned.1.call-start
  80.7 75.9 %all-gather.3.cloned.1.call-done = f32[512,2,2688]{0,2,1:T(8,128)} async-done(((f32[128,2,2688]{0,2,1:T(8,128)}), f32[512,2,2688]{0,2,1:T(8,128)}) %all-gather.3.cloned.1.call-update) | async-done | bytes 11010064 | tf_op jit(solution)/shard_map/all_gather | solution.py:19
  156.6 13.4 %reshape = f32[4,128,2,2688]{1,0,3,2:T(4,128)} reshape(f32[512,2,2688]{0,2,1:T(8,128)} %all-gather.3.cloned.1.call-done) | data formatting | bytes 22020096 | tf_op jit(solution)/shard_map/all_gather | solution.py:19
  170.0 27.6 %reduce_sum.9 = f32[128,2,2688]{0,2,1:T(8,128)S(1)} reduce(f32[4,128,2,2688]{1,0,3,2:T(4,128)} %reshape, f32[]{:T(128)} %constant.1.clone.1), dimensions={0}, to_apply=%region_0.0 | reduce | flops 2064384 | bytes 13762564 | tf_op jit(solution)/shard_map/reduce_sum | solution.py:19
  197.6 6.8 %fusion.9 = f32[128,2048]{1,0:T(8,128)} fusion(bf16[2688,2048]{1,0:T(8,128)(2,1)} %param.7, f32[128,2,2688]{0,2,1:T(8,128)S(1)} %reduce_sum.9), kind=kOutput, calls=%fused_computation.9 | convolution fusion | flops 1411350528 | bytes 14811136 | tf_op jit(solution)/shard_map/dot_general | solution.py:22
  204.4 0.0 reduce-scatter.2.cloned.1.call-update
  204.4 63.6 %reduce-scatter.2.cloned.1.call-done = f32[16,2048]{1,0:T(8,128)} async-done(((f32[128,2048]{1,0:T(8,128)}), f32[16,2048]{1,0:T(8,128)}) %reduce-scatter.2.cloned.1.call-update) | async-done | bytes 131088 | tf_op jit(solution)/shard_map/reduce_scatter | solution.py:21
  268.0 1.5 convert_element_type.7
Async XLA Ops:
  6.5 150.1 %all-gather.3.cloned.1.call-start = ((), (), s32[]{:S(2)}) async-start(), calls=%async_computation.2 | async-start | bytes 13762560 | tf_op jit(solution)/shard_map/all_gather | solution.py:19
  80.7 187.3 %reduce-scatter.2.cloned.1.call-start = ((), (), s32[]{:S(2)}) async-start(), calls=%async_computation.1 | async-start | bytes 1179648 | tf_op jit(solution)/shard_map/reduce_scatter | solution.py:21
Sparse Core Ops, SparseCore 0:
  80.8 75.7 all-gather.2
  204.6 63.4 reduce-scatter.1
